TPU v7x, 128 devices: a whole 4x4x4 slice. The times are simulated.
128 devices in a mesh: rep: 32 (over x, y, z_lo), tp: 4 (over z_hi, core).
Axes of the slice: x: 4, y: 4, z: 4 (z_hi: 2, z_lo: 2; z = z_hi * 2 + z_lo), core: 2. Of those that a mesh axis runs over, the one named last changes fastest.
Arguments:
- step_index: int32 [1], replicated, may hold values from 0 to 5
- inputs: bfloat16 [16384, 5120], P(('rep', 'tp')), may hold values from -6 to 6
- grad_out: bfloat16 [16384, 5120], P(('rep', 'tp')), may hold values from -6 to 6
- params: float32 [32, 3, 224, 5120], P('rep', None, 'tp'), may hold values from -0.078125 to 0.078125
- first_moment: float32 [32, 3, 224, 5120], P('rep', None, 'tp'), may hold values from -24 to 24
- second_moment: float32 [32, 3, 224, 5120], P('rep', None, 'tp'), may hold values from 16 to 1024
Outputs:
- new_params: float32 [32, 3, 224, 5120], P('rep', None, 'tp')
- new_first: float32 [32, 3, 224, 5120], P('rep', None, 'tp')
- new_second: float32 [32, 3, 224, 5120], P('rep', None, 'tp')
- input_grad: bfloat16 [16384, 5120], P(('rep', 'tp'))
All inputs are finite; a program needn't handle non-finite values.
Results may differ from a plain program's by a relative error of at most 0.0072.
Values may be sent and summed in bfloat16 or wider, within the bound.
A program may use at most 128 MiB of HBM per device.

v0:
```python
import functools
import jax
import jax.numpy as jnp
from jax import lax
from jax.experimental import pallas as pl
from jax.experimental.pallas import tpu as pltpu
from jax.sharding import PartitionSpec as P

CHUNK = 512
HALF = CHUNK // 2
WIDE = CHUNK + HALF
SLAB = 16
LAG = 2
MESH = pl.DeviceIdType.MESH
BF16 = jnp.bfloat16
F32 = jnp.float32
NT = (((1,), (1,)), ((), ()))
NN = (((1,), (0,)), ((), ()))
TN = (((0,), (0,)), ((), ()))


def dot(a, b, dims):
    return lax.dot_general(a, b, dims, preferred_element_type=F32)


def window_kernel(
    by,
    scale_ref, x_ref, g_ref, p_ref, m_ref, v_ref,
    np_ref, nm_ref, nv_ref, ig_ref,
    xb, gb, pb, mb, vb, w_own, w_rem, g_send, g_recv, u_send, u_recv,
    ig_send, ig_recv, ig_out, acc_a, acc_b, grad,
    d_own, d_rem, h_own, h_rem,
    p_sem, m_sem, v_sem, x_sem, g_sem,
    xs_sem, xr_sem, gs_sem, gr_sem,
    ws_sem, wr_sem, ds_sem, dr_sem, us_sem, ur_sem, is_sem, ir_sem,
    po_sem, mo_sem, vo_sem, io_sem,
):
    n_rep = lax.axis_size("rep")
    rep = lax.axis_index("rep")
    tp = lax.axis_index("tp")
    core = lax.rem(tp, 2)
    z_peer = (rep, lax.rem(tp + 2, 4))
    twin = (rep, tp + 1 - 2 * core)
    after = (lax.rem(rep + by, n_rep), tp)
    before = (lax.rem(rep + n_rep - by, n_rep), tp)

    tok, width = x_ref.shape
    hid = p_ref.shape[2]
    pair = 2 * hid
    count = width // CHUNK
    mine = pl.multiple_of(core * tok, tok)
    other = pl.multiple_of((1 - core) * tok, tok)

    def parts(hbm, buf, j):
        whole = pl.ds(pl.multiple_of(j * CHUNK, CHUNK), CHUNK)
        left = pl.ds(pl.multiple_of(j * CHUNK, HALF), HALF)
        right = pl.ds(pl.multiple_of(j * CHUNK + HALF, HALF), HALF)
        return [
            (hbm.at[0, 0, :, whole], buf.at[j, pl.ds(0, hid), pl.ds(0, CHUNK)]),
            (hbm.at[0, 1, :, whole], buf.at[j, pl.ds(hid, hid), pl.ds(0, CHUNK)]),
            (hbm.at[0, 2, :, left], buf.at[j, pl.ds(0, hid), pl.ds(CHUNK, HALF)]),
            (hbm.at[0, 2, :, right], buf.at[j, pl.ds(hid, hid), pl.ds(CHUNK, HALF)]),
        ]

    def load(hbm, buf, sem, j):
        for a, b in parts(hbm, buf, j):
            pltpu.make_async_copy(a, b, sem.at[j]).start()

    def store(hbm, buf, sem, j):
        for a, b in parts(hbm, buf, j):
            pltpu.make_async_copy(b, a, sem.at[j]).start()

    def wait_chunk(buf, sem, j):
        pltpu.make_async_copy(buf.at[j], buf.at[j], sem.at[j]).wait()

    def cols(j):
        return pl.ds(pl.multiple_of(j * CHUNK, CHUNK), CHUNK)

    def tokens_in(hbm, buf, sem, j):
        return pltpu.make_async_copy(
            hbm.at[:, cols(j)], buf.at[j, pl.ds(mine, tok), :], sem.at[j])

    def tokens_over(hbm, buf, s_sem, r_sem, j):
        return pltpu.make_async_remote_copy(
            src_ref=hbm.at[:, cols(j)], dst_ref=buf.at[j, pl.ds(mine, tok), :],
            send_sem=s_sem.at[j], recv_sem=r_sem.at[j],
            device_id=twin, device_id_type=MESH)

    def send(src, dst, s_sem, r_sem, device, j):
        return pltpu.make_async_remote_copy(
            src_ref=src.at[j], dst_ref=dst.at[j],
            send_sem=s_sem.at[j], recv_sem=r_sem.at[j],
            device_id=device, device_id_type=MESH)

    def loop(body):
        def step(j, carry):
            body(j)
            return carry
        lax.fori_loop(0, count, step, 0)

    barrier = pltpu.get_barrier_semaphore()
    for device in (z_peer, twin, before):
        pl.semaphore_signal(barrier, inc=1, device_id=device, device_id_type=MESH)

    loop(lambda j: load(p_ref, pb, p_sem, j))

    def token_loads(j):
        tokens_in(x_ref, xb, x_sem, j).start()
        tokens_in(g_ref, gb, g_sem, j).start()

    loop(token_loads)
    pl.semaphore_wait(barrier, 3)

    def send_weights(j):
        wait_chunk(pb, p_sem, j)
        w_own[j] = pb[j].astype(BF16)
        send(w_own, w_rem, ws_sem, wr_sem, z_peer, j).start()
        tokens_over(x_ref, xb, xs_sem, xr_sem, j).start()
        tokens_over(g_ref, gb, gs_sem, gr_sem, j).start()

    loop(send_weights)

    def moment_loads(j):
        load(m_ref, mb, m_sem, j)
        load(v_ref, vb, v_sem, j)

    loop(moment_loads)

    def project(w, j):
        acc_a[...] += dot(w[j, :, pl.ds(0, CHUNK)], xb[j], NT)
        down = w[j, :, pl.ds(CHUNK, HALF)]
        top = dot(down[: hid + 8], gb[j, :, pl.ds(0, HALF)], NT)
        low = dot(down[hid - 8:], gb[j, :, pl.ds(HALF, HALF)], NT)
        acc_b[...] += top[:hid] + low[8:]

    def start_sums():
        acc_a[...] = jnp.zeros_like(acc_a)
        acc_b[...] = jnp.zeros_like(acc_b)

    def finish_hidden(d_ref, h_ref):
        pre_gate = acc_a[pl.ds(0, hid), :]
        pre_up = acc_a[pl.ds(hid, hid), :]
        back = acc_b[...]
        s = jax.nn.sigmoid(pre_gate)
        silu = s * pre_gate
        pad = jnp.zeros((8, 2 * tok), F32)
        h_ref[...] = jnp.concatenate([silu * pre_up, pad], axis=0).astype(BF16)
        d_gate = back * pre_up * s * (1.0 + pre_gate * (1.0 - s))
        d_ref[...] = jnp.concatenate([d_gate, back * silu], axis=0).astype(BF16)

    def project_own(j):
        tokens_in(x_ref, xb, x_sem, j).wait()
        tokens_in(g_ref, gb, g_sem, j).wait()
        tokens_over(x_ref, xb, xs_sem, xr_sem, j).wait_recv()
        tokens_over(g_ref, gb, gs_sem, gr_sem, j).wait_recv()
        project(w_own, j)

    start_sums()
    loop(project_own)
    finish_hidden(d_own, h_own)

    def project_rem(j):
        send(w_own, w_rem, ws_sem, wr_sem, z_peer, j).wait_recv()
        project(w_rem, j)

    start_sums()
    loop(project_rem)
    finish_hidden(d_rem, h_rem)

    def gradient(d_ref, h_ref, j):
        first = dot(d_ref[...], xb[j], NN)
        last = dot(h_ref[...], gb[j], NN)[:hid]
        return first, jnp.concatenate([last[:, :HALF], last[:, HALF:]], axis=0)

    def send_gradients(j):
        first, last = gradient(d_rem, h_rem, j)
        g_send[j, :, pl.ds(0, CHUNK)] = first.astype(BF16)
        g_send[j, :, pl.ds(CHUNK, HALF)] = last.astype(BF16)
        send(g_send, g_recv, ds_sem, dr_sem, z_peer, j).start()

    loop(send_gradients)

    def back_project(rows, j):
        return dot(d_own[:, pl.ds(rows, tok)], w_own[j, :, pl.ds(0, CHUNK)], TN) + dot(
            d_rem[:, pl.ds(rows, tok)], w_rem[j, :, pl.ds(0, CHUNK)], TN)

    scale_first = scale_ref[0]
    scale_second = scale_ref[1]

    def adam(j):
        first, last = gradient(d_own, h_own, j)
        grad[:, pl.ds(0, CHUNK)] = first
        grad[:, pl.ds(CHUNK, HALF)] = last
        send(g_send, g_recv, ds_sem, dr_sem, z_peer, j).wait_recv()
        wait_chunk(mb, m_sem, j)
        wait_chunk(vb, v_sem, j)

        def slab(i, carry):
            rows = pl.ds(pl.multiple_of(i * SLAB, SLAB), SLAB)
            gr = grad[rows, :] + g_recv[j, rows, :].astype(F32)
            first_new = 0.9 * mb[j, rows, :] + 0.1 * gr
            second_new = 0.95 * vb[j, rows, :] + 0.05 * gr * gr
            mb[j, rows, :] = first_new
            vb[j, rows, :] = second_new
            weights = pb[j, rows, :]
            update = first_new * scale_first / (jnp.sqrt(second_new * scale_second) + 1e-08)
            updated = weights - 0.01 * (update + 0.1 * weights)
            pb[j, rows, :] = updated
            u_send[j, rows, :] = updated.astype(BF16)
            return carry

        lax.fori_loop(0, pair // SLAB, slab, 0)

    def average(j):
        send(u_send, u_recv, us_sem, ur_sem, after, j).wait_recv()
        pb[j] = 0.5 * (pb[j] + u_recv[j].astype(F32))
        store(np_ref, pb, po_sem, j)

    def input_gradient(j):
        send(ig_send, ig_recv, is_sem, ir_sem, twin, j).wait_recv()
        ig_out[j] = (back_project(mine, j) + ig_recv[j]).astype(BF16)
        pltpu.make_async_copy(ig_out.at[j], ig_ref.at[:, cols(j)], io_sem.at[j]).start()

    def update_step(j):
        adam(j)
        send(u_send, u_recv, us_sem, ur_sem, after, j).start()
        store(nm_ref, mb, mo_sem, j)
        store(nv_ref, vb, vo_sem, j)
        ig_send[j] = back_project(other, j)
        send(ig_send, ig_recv, is_sem, ir_sem, twin, j).start()

        @pl.when(j >= 1)
        def _():
            input_gradient(j - 1)

        @pl.when(j >= LAG)
        def _():
            average(j - LAG)

    loop(update_step)
    input_gradient(count - 1)
    for j in range(count - LAG, count):
        average(j)

    def drain(j):
        send(w_own, w_rem, ws_sem, wr_sem, z_peer, j).wait_send()
        tokens_over(x_ref, xb, xs_sem, xr_sem, j).wait_send()
        tokens_over(g_ref, gb, gs_sem, gr_sem, j).wait_send()
        send(g_send, g_recv, ds_sem, dr_sem, z_peer, j).wait_send()
        send(u_send, u_recv, us_sem, ur_sem, after, j).wait_send()
        send(ig_send, ig_recv, is_sem, ir_sem, twin, j).wait_send()
        wait_chunk(pb, po_sem, j)
        wait_chunk(mb, mo_sem, j)
        wait_chunk(vb, vo_sem, j)
        pltpu.make_async_copy(ig_out.at[j], ig_ref.at[:, cols(j)], io_sem.at[j]).wait()

    loop(drain)


def window(by, collective_id, scales, inputs, grad_out, params, first, second):
    tok, width = inputs.shape
    hid = params.shape[2]
    pair = 2 * hid
    count = width // CHUNK
    anywhere = pl.BlockSpec(memory_space=pl.ANY)
    block = pltpu.VMEM((count, pair, WIDE), BF16)
    wide = pltpu.VMEM((count, pair, WIDE), F32)
    token = pltpu.VMEM((count, 2 * tok, CHUNK), BF16)
    partial = pltpu.VMEM((count, tok, CHUNK), F32)
    like = jax.ShapeDtypeStruct(params.shape, F32)
    return pl.pallas_call(
        functools.partial(window_kernel, by),
        out_shape=[like, like, like, jax.ShapeDtypeStruct(inputs.shape, BF16)],
        in_specs=[pl.BlockSpec(memory_space=pltpu.SMEM)] + [anywhere] * 5,
        out_specs=[anywhere] * 4,
        scratch_shapes=[token] * 2 + [wide] * 3 + [block] * 6 + [partial] * 2
        + [pltpu.VMEM((count, tok, CHUNK), BF16)]
        + [pltpu.VMEM((pair, 2 * tok), F32), pltpu.VMEM((hid, 2 * tok), F32)]
        + [pltpu.VMEM((pair, WIDE), F32)]
        + [pltpu.VMEM((pair, 2 * tok), BF16)] * 2
        + [pltpu.VMEM((hid + 8, 2 * tok), BF16)] * 2
        + [pltpu.SemaphoreType.DMA((count,))] * 21,
        compiler_params=pltpu.CompilerParams(
            collective_id=collective_id, has_side_effects=True,
            vmem_limit_bytes=56 * 2 ** 20),
        name=f"window_by_{by}",
    )(scales, inputs, grad_out, params, first, second)


def copy_kernel(n, *refs):
    sources, targets, sem = refs[:n], refs[n: 2 * n], refs[2 * n]
    copies = []
    for source, target in zip(sources, targets):
        if len(source.shape) == 4:
            pieces = [(source.at[0, i], target.at[0, i]) for i in range(source.shape[1])]
        else:
            pieces = [(source, target)]
        for a, b in pieces:
            copies.append(pltpu.make_async_copy(a, b, sem.at[len(copies)]))
    for copy in copies:
        copy.start()
    for copy in copies:
        copy.wait()


def hand_over(arrays):
    n = len(arrays)
    anywhere = pl.BlockSpec(memory_space=pl.ANY)
    return pl.pallas_call(
        functools.partial(copy_kernel, n),
        out_shape=[jax.ShapeDtypeStruct(a.shape, a.dtype) for a in arrays],
        in_specs=[anywhere] * n,
        out_specs=[anywhere] * n,
        scratch_shapes=[pltpu.SemaphoreType.DMA((3 * n,))],
        name="hand_over",
    )(*arrays)


def make_branch(bit):

    def run(*values):
        return tuple(hand_over(window(1 << bit, bit, *values)))

    return run


def per_device(step_index, inputs, grad_out, params, first_moment, second_moment):
    bits = lax.axis_size("rep").bit_length() - 1
    count_now = (step_index[0] + 1).astype(F32)
    fixes = 1.0 - jnp.power(jnp.array([0.9, 0.95], F32), count_now)
    branches = [make_branch(bit) for bit in range(bits)]
    return lax.switch(
        step_index[0] % bits, branches, 1.0 / fixes,
        inputs, grad_out, params, first_moment, second_moment)


def solution(mesh):
    return jax.shard_map(
        per_device,
        mesh=mesh,
        in_specs=(
            P(),
            P(("rep", "tp"), None),
            P(("rep", "tp"), None),
            P("rep", None, "tp", None),
            P("rep", None, "tp", None),
            P("rep", None, "tp", None),
        ),
        out_specs=(
            P("rep", None, "tp", None),
            P("rep", None, "tp", None),
            P("rep", None, "tp", None),
            P(("rep", "tp"), None),
        ),
        check_vma=False,
    )
```

profile of v0, /device:TPU:16, one launch (start us, length us, event | category | flops | bytes accessed | tf_op | source)
XLA Modules:
  0.0 484.2 jit_solution(14421220615129793746)
XLA Ops:
  1.3 482.9 %conditional.1 = ((f32[1,3,56,5120]{3,2,1,0:T(8,128)}, f32[1,3,56,5120]{3,2,1,0:T(8,128)}, f32[1,3,56,5120]{3,2,1,0:T(8,128)}, bf16[128,5120]{1,0:T(8,128)(2,1)})) conditional(s32[]{:T(128)} %clamp.3, (f32[2]{0:T(128)S(1)}, bf16[128,5120]{1,0:T(8,128)(2,1)}, bf16[128,5120]{1,0:T(8,128)(2,1)}, ...), branch_computations={%region_0.1_spmd.clone, %region_1.2_spmd.clone, %region_2.3_spmd.c... | conditional | flops 4 | bytes 44 | solution.py:332
  1.3 1.2 fusion.scale_ref
  2.5 128.1 %window_by_1.1 = (f32[1,3,56,5120]{3,2,1,0:T(8,128)}, f32[1,3,56,5120]{3,2,1,0:T(8,128)}, f32[1,3,56,5120]{3,2,1,0:T(8,128)}, bf16[128,5120]{1,0:T(8,128)(2,1)}) custom-call(f32[2]{0:T(128)} %fusion.scale_ref, bf16[128,5120]{1,0:T(8,128)(2,1)} %get-tuple-element.248.x_ref, bf16[128,5120]{1,0:T(8,128)(2,1)} %get-tuple-element.249.g_ref, ...), custom_call_target="tpu_custom_call" | custom-call | tf_op jit(solution)/shard_map/cond/branch_0_fun/window_by_1/pallas_call | solution.py:271
  130.6 353.6 %hand_over.5 = (f32[1,3,56,5120]{3,2,1,0:T(8,128)}, f32[1,3,56,5120]{3,2,1,0:T(8,128)}, f32[1,3,56,5120]{3,2,1,0:T(8,128)}, bf16[128,5120]{1,0:T(8,128)(2,1)}) custom-call(f32[1,3,56,5120]{3,2,1,0:T(8,128)} %get-tuple-element.238.refs_0_, f32[1,3,56,5120]{3,2,1,0:T(8,128)} %get-tuple-element.239.refs_1_, f32[1,3,56,5120]{3,2,1,0:T(8,128)} %get-tuple-element.240.refs_2_, ...), custom_call_target="tpu_custom_call" | custom-call | tf_op jit(solution)/shard_map/cond/branch_0_fun/hand_over/pallas_call | solution.py:309
  (1 shorter events, 0.0 us)
where the time goes:
time: 484 us
  Pallas kernels  482 us (100%)
    pallas_call x1, Pallas kernels, hand_over(): pl.pallas_call(functools.partial(copy_kernel, n), out_shape=[jax.ShapeDty...  354 us
    pallas_call x1, Pallas kernels, window(): pl.pallas_call(functools.partial(window_kernel, by), out_shape=[like, lik...  128 us

commit v1 on v0

--- a/solution.py
+++ b/solution.py
@@ -282,7 +282,7 @@
         + [pltpu.SemaphoreType.DMA((count,))] * 21,
         compiler_params=pltpu.CompilerParams(
             collective_id=collective_id, has_side_effects=True,
-            vmem_limit_bytes=56 * 2 ** 20),
+            vmem_limit_bytes=40 * 2 ** 20),
         name=f"window_by_{by}",
     )(scales, inputs, grad_out, params, first, second)
 
@@ -312,6 +312,7 @@
         in_specs=[anywhere] * n,
         out_specs=[anywhere] * n,
         scratch_shapes=[pltpu.SemaphoreType.DMA((3 * n,))],
+        compiler_params=pltpu.CompilerParams(vmem_limit_bytes=16 * 2 ** 20),
         name="hand_over",
     )(*arrays)
 

time: 484 us -> 134 us (0.28)
  Pallas kernels: 482 us -> 132 us
    pallas_call x1, Pallas kernels: 354 us -> 4.4 us  [hand_over(): pl.pallas_call(functools.partial(copy_kernel, n), out_shape=[jax.ShapeDty...]
where the time goes in v1:
time: 134 us
  Pallas kernels  132 us (99%)
    pallas_call x1, Pallas kernels, window(): pl.pallas_call(functools.partial(window_kernel, by), out_shape=[like, lik...  128 us
    pallas_call x1, Pallas kernels, hand_over(): pl.pallas_call(functools.partial(copy_kernel, n), out_shape=[jax.ShapeDty...  4.4 us

profile of v1, /device:TPU:16, one launch (start us, length us, event | category | flops | bytes accessed | tf_op | source)
XLA Modules:
  0.0 134.0 jit_solution(11186676621913471280)
XLA Ops:
  1.3 132.7 %conditional.1 = ((f32[1,3,56,5120]{3,2,1,0:T(8,128)}, f32[1,3,56,5120]{3,2,1,0:T(8,128)}, f32[1,3,56,5120]{3,2,1,0:T(8,128)}, bf16[128,5120]{1,0:T(8,128)(2,1)})) conditional(s32[]{:T(128)} %clamp.3, (f32[2]{0:T(128)S(1)}, bf16[128,5120]{1,0:T(8,128)(2,1)}, bf16[128,5120]{1,0:T(8,128)(2,1)}, ...), branch_computations={%region_0.1_spmd.clone, %region_1.2_spmd.clone, %region_2.3_spmd.c... | conditional | flops 4 | bytes 44 | solution.py:333
  1.3 0.7 fusion.scale_ref
  2.0 127.5 %window_by_1.1 = (f32[1,3,56,5120]{3,2,1,0:T(8,128)S(1)}, f32[1,3,56,5120]{3,2,1,0:T(8,128)S(1)}, f32[1,3,56,5120]{3,2,1,0:T(8,128)S(1)}, bf16[128,5120]{1,0:T(8,128)(2,1)S(1)}) custom-call(f32[2]{0:T(128)S(1)} %fusion.scale_ref, bf16[128,5120]{1,0:T(8,128)(2,1)} %get-tuple-element.248.x_ref, bf16[128,5120]{1,0:T(8,128)(2,1)} %get-tuple-element.249.g_ref, ...), custom_call_target="tpu_custom_call" | custom-call | tf_op jit(solution)/shard_map/cond/branch_0_fun/window_by_1/pallas_call | solution.py:271
  129.5 4.4 %hand_over.5 = (f32[1,3,56,5120]{3,2,1,0:T(8,128)}, f32[1,3,56,5120]{3,2,1,0:T(8,128)}, f32[1,3,56,5120]{3,2,1,0:T(8,128)}, bf16[128,5120]{1,0:T(8,128)(2,1)}) custom-call(f32[1,3,56,5120]{3,2,1,0:T(8,128)S(1)} %get-tuple-element.238.refs_0_, f32[1,3,56,5120]{3,2,1,0:T(8,128)S(1)} %get-tuple-element.239.refs_1_, ...), custom_call_target="tpu_custom_call" | custom-call | tf_op jit(solution)/shard_map/cond/branch_0_fun/hand_over/pallas_call | solution.py:309
  (1 shorter events, 0.0 us)
